TPU v7x, 256 devices: a whole 4x4x8 slice. The times are simulated.
256 devices in a mesh: section: 64 (over y_lo, z, x), tensor: 4 (over y_hi, core).
Axes of the slice: x: 4, y: 4 (y_hi: 2, y_lo: 2; y = y_hi * 2 + y_lo), z: 8, core: 2. Of those that a mesh axis runs over, the one named last changes fastest.
Arguments:
- acts: bfloat16 [64, 512, 4096], P('section', 'tensor'), may hold values from -6 to 6
- norm_gain: float32 [64, 4096], P('section'), may hold values from 0.1 to 1.9
- w_qkv: bfloat16 [64, 4096, 3072], P('section', None, 'tensor'), may hold values from -0.09375 to 0.09375
- w_out: bfloat16 [64, 2048, 4096], P('section', 'tensor'), may hold values from -0.75 to 0.75
- kv_cache: bfloat16 [64, 1024, 1024], P('section', None, 'tensor')
- block_index: int32 [64], P('section'), may hold values from 0 to 63, as said below
- valid_len: int32 [64], P('section'), may hold values from 0 to 1024, as said below
Outputs:
- passed: bfloat16 [64, 512, 4096], P('section', 'tensor')
Inputs may be any that keep to these rules, and one draw needn't show every extreme that they name: `block_index`: some section holds block 0 and some the last block of the prompt. `valid_len`: some section has no live cached positions and some has all.
All inputs are finite; a program needn't handle non-finite values.
Results may differ from a plain program's by a relative error of at most 0.029.
Values may be sent and summed in bfloat16 or wider, within the bound.
A program may use at most 128 MiB of HBM per device.

v0:
```python
import math

import jax
import jax.numpy as jnp
from jax import lax
from jax.sharding import PartitionSpec as P

GROUP = 4


def passed_along(shard, axis, by):
    length = lax.axis_size(axis)
    return lax.ppermute(shard, axis, [(i, (i + by) % length) for i in range(length)])


def rotate(table, positions):
    half_dim = table.shape[-1] // 2
    inv_freq = jnp.exp(
        -jnp.log(jnp.float32(500000.0))
        * (2.0 * jnp.arange(half_dim, dtype=jnp.float32) / (2 * half_dim))
    )
    angles = positions.astype(jnp.float32)[:, None] * inv_freq[None, :]
    shape = (table.shape[0],) + (1,) * (table.ndim - 2) + (half_dim,)
    cosine = jnp.cos(angles).reshape(shape)
    sine = jnp.sin(angles).reshape(shape)
    first = table[..., :half_dim]
    second = table[..., half_dim:]
    return jnp.concatenate([first * cosine - second * sine, second * cosine + first * sine], -1)


def body(acts, norm_gain, w_qkv, w_out, kv_cache, block_index, valid_len):
    tok_rows = acts[0]
    residual = tok_rows.astype(jnp.float32)
    normed = (
        residual
        * lax.rsqrt(jnp.mean(residual * residual, -1, keepdims=True) + 1e-05)
        * norm_gain[0][None, :]
    ).astype(jnp.bfloat16)
    weight_in = w_qkv[0]
    qkv = jnp.dot(
        lax.all_gather(normed, "tensor", axis=0, tiled=True),
        weight_in,
        preferred_element_type=jnp.float32,
    )
    stored = kv_cache[0]
    head_size = stored.shape[1] // 2
    query_cols = GROUP * head_size
    row_count = qkv.shape[0]
    positions = block_index[0] * row_count + jnp.arange(row_count, dtype=jnp.int32)
    queries = rotate(qkv[:, :query_cols].reshape(row_count, GROUP, head_size), positions).astype(
        jnp.bfloat16
    )
    queries = queries.reshape(row_count * GROUP, head_size)
    new_keys = rotate(qkv[:, query_cols : query_cols + head_size], positions).astype(jnp.bfloat16)
    new_values = qkv[:, query_cols + head_size :].astype(jnp.bfloat16)
    cached_keys = stored[:, :head_size]
    cached_values = stored[:, head_size:]
    score_scale = 1.0 / math.sqrt(head_size)
    s_cache = (
        jnp.einsum("qd,kd->qk", queries, cached_keys, preferred_element_type=jnp.float32)
        * score_scale
    )
    live_mask = (jnp.arange(stored.shape[0], dtype=jnp.int32) < valid_len[0])[None, :]
    s_cache = jnp.where(live_mask, s_cache, -jnp.inf)
    s_own = (
        jnp.einsum("qd,kd->qk", queries, new_keys, preferred_element_type=jnp.float32) * score_scale
    )
    token_of_row = jnp.arange(row_count * GROUP) // GROUP
    causal = token_of_row[:, None] >= jnp.arange(row_count)[None, :]
    s_own = jnp.where(causal, s_own, -jnp.inf)
    row_max = jnp.maximum(jnp.max(s_cache, -1, keepdims=True), jnp.max(s_own, -1, keepdims=True))
    e_cache = jnp.exp(s_cache - row_max)
    e_own = jnp.exp(s_own - row_max)
    softmax_total = jnp.sum(e_cache, -1, keepdims=True) + jnp.sum(e_own, -1, keepdims=True)
    p_cache = (e_cache / softmax_total).astype(jnp.bfloat16)
    p_own = (e_own / softmax_total).astype(jnp.bfloat16)
    attn = jnp.dot(p_cache, cached_values, preferred_element_type=jnp.float32)
    attn = (attn + jnp.dot(p_own, new_values, preferred_element_type=jnp.float32)).astype(
        jnp.bfloat16
    )
    attn = attn.reshape(row_count, query_cols)
    weight_out = w_out[0]
    delta = lax.psum_scatter(
        jnp.dot(attn, weight_out, preferred_element_type=jnp.float32),
        "tensor",
        scatter_dimension=0,
        tiled=True,
    )
    moved = passed_along((residual + delta).astype(jnp.bfloat16), "section", 1)
    return moved[None]


def solution(mesh):
    in_specs = (
        P("section", "tensor", None),
        P("section", None),
        P("section", None, "tensor"),
        P("section", "tensor", None),
        P("section", None, "tensor"),
        P("section"),
        P("section"),
    )
    out_specs = P("section", "tensor", None)
    return jax.shard_map(body, mesh=mesh, in_specs=in_specs, out_specs=out_specs, check_vma=False)
```

profile of v0, /device:TPU:1, one launch (start us, length us, event | category | flops | bytes accessed | tf_op | source)
XLA Modules:
  0.0 207.2 jit_solution(1327493296639624789)
XLA Ops:
  6.5 0.0 all-gather.2.cloned.1.call-start
  6.5 1.5 fusion.9
  8.1 2.5 %fusion.11 = bf16[128,4096]{1,0:T(8,128)(2,1)} fusion(bf16[1,128,4096]{2,1,0:T(8,128)(2,1)} %param.7, f32[4096]{0:T(1024)} %bitcast.28, f32[128]{0:T(128)S(1)} %add_rsqrt_fusion), kind=kLoop, calls=%fused_computation.22 | loop fusion | flops 2097152 | bytes 2114048 | tf_op jit(solution)/shard_map/convert_element_type | solution.py:38
  10.6 0.0 all-gather.2.cloned.1.call-update
  10.6 0.0 reduce-scatter.2.cloned.1.call-start
  12.0 44.1 %all-gather.2.cloned.1.call-done = bf16[512,4096]{1,0:T(8,128)(2,1)} async-done(((bf16[128,4096]{1,0:T(8,128)(2,1)}), bf16[512,4096]{1,0:T(8,128)(2,1)}) %all-gather.2.cloned.1.call-update) | async-done | bytes 4194320 | tf_op jit(solution)/shard_map/all_gather | solution.py:41
  56.1 7.0 %fusion.2 = f32[512,768]{1,0:T(8,128)S(1)} fusion(bf16[512,4096]{1,0:T(8,128)(2,1)} %all-gather.2.cloned.1.call-done, bf16[1,4096,768]{2,1,0:T(8,128)(2,1)} %param.9), kind=kOutput, calls=%fused_computation.5 | convolution fusion | flops 3221225472 | bytes 12058624 | tf_op jit(solution)/shard_map/dot_general | solution.py:40
  63.1 0.0 copy-start.1
  63.1 1.1 copy-done.1
  64.3 0.0 copy-start.2
  64.3 0.1 slice.36
  64.4 0.4 reshape.111
  64.8 2.2 %subtract_convert_fusion.1 = (bf16[512,64]{1,0:T(8,128)(2,1)S(1)}, bf16[512,64]{1,0:T(8,128)(2,1)S(1)}, f32[512,64]{1,0:T(8,128)S(1)}, f32[512,64]{1,0:T(8,128)S(1)}) fusion(f32[512,768]{1,0:T(8,128)} %copy-done.1, f32[64]{0:T(128)S(1)} %multiply_exponential_fusion, f32[512]{0:T(512)S(1)} %add_convert_fusion.2), kind=kLoop, calls=%fused_computation.34 | loop fusion | flops 294912 | bytes 657664 | tf_op jit(solution)/shard_map/convert.2
  67.0 0.8 subtract_convert_fusion
  67.8 0.0 copy-done.2
  67.9 1.4 fusion
  69.3 1.2 fusion.26
  70.5 0.6 fusion.7
  71.1 2.7 %fusion.1 = f32[2048]{0:T(1024)S(1)} fusion(f32[2048,1024]{0,1:T(8,128)S(1)} %get-tuple-element.12, f32[2048]{0:T(1024)S(1)} %max.8, pred[1024]{0:T(1024)(128)(4,1)S(1)} %iota_compare_fusion.1), kind=kLoop, calls=%fused_computation.4 | loop fusion | flops 8386560 | bytes 8406016 | tf_op jit(solution)/shard_map/reduce_sum | solution.py:74
  73.8 2.4 %fusion.6 = f32[2048,128]{1,0:T(8,128)S(1)} fusion(f32[2048,1024]{0,1:T(8,128)S(1)} %get-tuple-element.12, f32[2048]{0:T(1024)S(1)} %add.54, f32[2048]{0:T(1024)S(1)} %max.8, pred[1024]{0:T(1024)(128)(4,1)S(1)} %iota_compare_fusion.1, bf16[1024,256]{1,0:T(8,128)(2,1)S(1)} %bitcast.27), kind=kOutput, calls=%fused_computation.13 | convolution fusion | flops 547356672 | bytes 9716736 | tf_op jit(solution)/shard_map/dot_general | solution.py:77
  76.2 2.0 fusion.8
  78.2 0.3 reshape.112
  78.6 7.8 %fusion.4 = f32[512,4096]{1,0:T(8,128)} fusion(bf16[512,512]{1,0:T(8,128)(2,1)S(1)} %reshape.112, bf16[1,512,4096]{2,1,0:T(8,128)(2,1)} %param.10), kind=kOutput, calls=%fused_computation.7 | convolution fusion | flops 2147483648 | bytes 13107200 | tf_op jit(solution)/shard_map/dot_general | solution.py:84
  86.3 0.0 copy-start
  86.3 0.0 reduce-scatter.2.cloned.1.call-update
  86.3 82.9 %reduce-scatter.2.cloned.1.call-done = f32[128,4096]{1,0:T(8,128)} async-done(((f32[512,4096]{1,0:T(8,128)}), f32[128,4096]{1,0:T(8,128)}) %reduce-scatter.2.cloned.1.call-update) | async-done | bytes 2097168 | tf_op jit(solution)/shard_map/reduce_scatter | solution.py:83
  169.3 0.0 copy-done
  169.3 1.8 fusion.12
  171.1 1.3 collective-permute-start
  172.4 27.1 %collective-permute-done = bf16[128,4096]{1,0:T(8,128)(2,1)S(1)} collective-permute-done((bf16[128,4096]{1,0:T(8,128)(2,1)S(1)}, bf16[128,4096]{1,0:T(8,128)(2,1)S(1)}, u32[]{:S(2)}, u32[]{:S(2)}) %collective-permute-start) | collective-permute-done | bytes 1048608 | tf_op jit(solution)/shard_map/ppermute | solution.py:13
  199.4 1.0 copy.11
  (7 shorter events, 0.0 us)
Async XLA Ops:
  6.5 49.5 %all-gather.2.cloned.1.call-start = ((), (), s32[]{:S(2)}) async-start(), calls=%async_computation.1 | async-start | bytes 5242880 | tf_op jit(solution)/shard_map/all_gather | solution.py:41
  10.6 158.7 %reduce-scatter.2.cloned.1.call-start = ((), (), s32[]{:S(2)}) async-start(), calls=%async_computation.2 | async-start | bytes 10485760 | tf_op jit(solution)/shard_map/reduce_scatter | solution.py:83
  63.1 1.2 copy-start.1
  64.3 3.6 %copy-start.2 = (bf16[1,1024,256]{2,1,0:T(8,128)(2,1)S(1)}, bf16[1,1024,256]{2,1,0:T(8,128)(2,1)}, u32[]{:S(2)}) copy-start(bf16[1,1024,256]{2,1,0:T(8,128)(2,1)} %param.11) | copy-start | bytes 1572868
  86.3 83.0 %copy-start = (bf16[1,128,4096]{2,1,0:T(8,128)(2,1)S(1)}, bf16[1,128,4096]{2,1,0:T(8,128)(2,1)}, u32[]{:S(2)}) copy-start(bf16[1,128,4096]{2,1,0:T(8,128)(2,1)} %param.7) | copy-start | bytes 3145732
  171.1 28.3 %collective-permute-start = (bf16[128,4096]{1,0:T(8,128)(2,1)S(1)}, bf16[128,4096]{1,0:T(8,128)(2,1)S(1)}, u32[]{:S(2)}, u32[]{:S(2)}) collective-permute-start(bf16[128,4096]{1,0:T(8,128)(2,1)S(1)} %fusion.12), channel_id=1, source_target_pairs={{0,4},{4,8},{8,12},{12,16},{16,20},{20,24},{24,28},{28,32},{32,36}... | collective-permute-start | bytes 3145736 | tf_op jit(solution)/shard_map/ppermute | solution.py:13
Sparse Core Ops, SparseCore 0:
  10.7 45.2 all-gather.1
  86.5 82.7 reduce-scatter.1
where the time goes:
time: 208 us; the launch traced here: 207 us
  waiting for transfers between devices  154 us (74%)
  matrix products  21.8 us (10%)
  between operations  14.8 us (7%)
  other arithmetic  12.2 us (6%)
  local copies, waits for them, and re-layouts  2.94 us (1%)
    reduce_scatter x1, waiting for transfers between devices, body(): lax.psum_scatter(jnp.dot(attn, weight_out, preferred_element_type=jnp.flo...  82.9 us
    all_gather x1, waiting for transfers between devices, body(): lax.all_gather(normed, 'tensor', axis=0, tiled=True)  44.1 us
    ppermute x1, waiting for transfers between devices, passed_along(): lax.ppermute(shard, axis, [(i, (i + by) % length) for i in range(length)])  27.1 us
    dot_general x1, matrix products, body(): jnp.dot(attn, weight_out, preferred_element_type=jnp.float32)  7.76 us
    dot_general x1, matrix products, body(): jnp.dot(lax.all_gather(normed, 'tensor', axis=0, tiled=True), weight_in,...  7.03 us
  transfers between devices with their start and end apart: 3, of which 3 were waited for; matrix products, arithmetic and copies ran while one was open for 0% of the time, Pallas kernels for 0%

commit v1 on v0

v1 whole, which is shorter than its diff:
```python
import functools
import math

import jax
import jax.numpy as jnp
import numpy as np
from jax import lax
from jax.experimental import pallas as pl
from jax.experimental.pallas import tpu as pltpu
from jax.sharding import PartitionSpec as P

GROUP = 4
HD = 128
AG = 4
PIECE = 16
MESH = pl.DeviceIdType.MESH
F32 = jnp.float32
BF16 = jnp.bfloat16


def kernel(
    sections, bidx, vlen, freq, acts, gain, wqkv, wout, cache, out,
    a_v, g_v, nrm, wq, wo, kv, bias, ct, st, qb, kb, vb, att, res, base, snd, rcv, bsnd, brcv, fin,
    l_sem, ag_s, ag_r, mt_s, mt_r, fw_s, fw_r, wo_s, wo_r, at_s, at_r, rs_s, rs_r, bs_s, bs_r, x_s, x_r,
):
    rows, dim = a_v.shape
    wide = dim // 2
    chunk = rows // AG
    part_rows = rows // 2
    per = part_rows // PIECE
    half = sections // 2

    s = lax.axis_index("section")
    t = lax.axis_index("tensor")
    c = lax.rem(t, 2)
    hi = lax.div(t, 2)
    low = lax.rem(s, half)
    last = lax.div(low, half - 1)
    nxt = s - low + lax.rem(low + 1, half)
    prv = s - low + lax.rem(low + half - 1, half)
    oth = lax.rem(s + half, sections)
    mate = (s, 2 * hi + 1 - c)
    partner = (s, 2 * (1 - hi) + c)
    sum_dev = (lax.rem(s + half * last, sections), 2 * (1 - hi) + c)
    base_dev = (oth, t)
    special = last == 1

    def remote(src, dst, ss, rs, dev):
        return pltpu.make_async_remote_copy(
            src_ref=src, dst_ref=dst, send_sem=ss, recv_sem=rs, device_id=dev, device_id_type=MESH
        )

    mine = pl.ds(pl.multiple_of(c * wide, wide), wide)
    others = pl.ds(pl.multiple_of((1 - c) * wide, wide), wide)
    g_cp = pltpu.make_async_copy(gain, g_v, l_sem.at[AG])
    a_cp = [
        pltpu.make_async_copy(
            acts.at[0, pl.ds(j * chunk, chunk)], a_v.at[pl.ds(j * chunk, chunk)], l_sem.at[j]
        )
        for j in range(AG)
    ]
    a_cp[0].start()
    g_cp.start()
    for j in range(1, AG):
        a_cp[j].start()
    wq_cp = pltpu.make_async_copy(wqkv.at[0], wq, l_sem.at[AG + 1])
    kv_cp = pltpu.make_async_copy(cache.at[0], kv, l_sem.at[AG + 2])
    wo_cp = pltpu.make_async_copy(wout.at[0, :, mine], wo.at[0], l_sem.at[AG + 3])
    res_cp = pltpu.make_async_copy(acts.at[0, :, mine], res.at[c], l_sem.at[AG + 4])
    wq_cp.start()
    kv_cp.start()

    barrier = pltpu.get_barrier_semaphore()
    for dev in (
        partner, mate, (nxt, 2 * hi), (nxt, 2 * hi + 1), (prv, 2 * hi), (prv, 2 * hi + 1),
    ):
        pl.semaphore_signal(barrier, inc=1, device_id=dev, device_id_type=MESH)

    @pl.when(special)
    def _():
        for dev in (base_dev, sum_dev):
            pl.semaphore_signal(barrier, inc=1, device_id=dev, device_id_type=MESH)

    def ag_copy(j):
        r = pl.ds(j * chunk, chunk)
        return remote(nrm.at[c, r], nrm.at[2 + c, r], ag_s.at[j], ag_r.at[j], partner)

    def mate_copy(j):
        r = pl.ds(j * chunk, chunk)
        return remote(nrm.at[c, r], nrm.at[c, r], mt_s.at[j], mt_r.at[j], mate)

    def mate_arrival(j):
        r = pl.ds(j * chunk, chunk)
        return remote(nrm.at[1 - c, r], nrm.at[1 - c, r], mt_s.at[j], mt_r.at[j], mate)

    def fwd_copy(j):
        r = pl.ds(j * chunk, chunk)
        return remote(nrm.at[2 + c, r], nrm.at[2 + c, r], fw_s.at[j], fw_r.at[j], mate)

    def fwd_arrival(j):
        r = pl.ds(j * chunk, chunk)
        return remote(nrm.at[3 - c, r], nrm.at[3 - c, r], fw_s.at[j], fw_r.at[j], mate)

    def normalize(j):
        a_cp[j].wait()
        r = pl.ds(j * chunk, chunk)
        x = a_v[r, :].astype(F32)
        ms = jnp.mean(x * x, -1, keepdims=True)
        nrm[c, r, :] = (x * lax.rsqrt(ms + 1e-05) * g_v[...]).astype(BF16)

    g_cp.wait()
    normalize(0)
    pl.semaphore_wait(barrier, 6 + 2 * last)

    ag_copy(0).start()
    mate_copy(0).start()
    for j in range(1, AG):
        normalize(j)
        ag_copy(j).start()
        mate_copy(j).start()

    wo_cp.start()
    res_cp.start()
    wo_rm = remote(wout.at[0, :, others], wo.at[1], wo_s.at[0], wo_r.at[0], mate)
    res_rm = remote(acts.at[0, :, others], res.at[c], wo_s.at[1], wo_r.at[1], mate)
    res_in = remote(acts.at[0, :, mine], res.at[1 - c], wo_s.at[1], wo_r.at[1], mate)
    wo_rm.start()
    res_rm.start()

    kb[...] = jnp.zeros_like(kb)
    vb[...] = jnp.zeros_like(vb)
    lane = lax.broadcasted_iota(jnp.int32, (rows, HD), 1)
    sign = jnp.where(lane < HD // 2, -1.0, 1.0).astype(F32)
    row = lax.broadcasted_iota(jnp.int32, (rows, HD), 0)

    def tables(k, _):
        rel, b = lax.div(k, 2), lax.rem(k, 2)
        side = hi + rel - 2 * hi * rel
        pos = bidx[0] * (4 * rows) + (2 * side + b) * rows + row
        angle = pos.astype(F32) * freq[...]
        turns = jnp.floor(angle * np.float32(1.0 / (2.0 * math.pi)) + 0.5)
        small = ((angle - turns * TURN[0]) - turns * TURN[1]) - turns * TURN[2]
        r = pl.ds(pl.multiple_of(k * rows, rows), rows)
        ct[r, :] = jnp.cos(small)
        st[r, :] = jnp.sin(small) * sign
        return 0

    lax.fori_loop(0, 4, tables, 0)
    key_id = lax.broadcasted_iota(jnp.int32, bias.shape, 1)
    bias[...] = jnp.where(key_id < vlen[0], 0.0, -jnp.inf).astype(F32)

    def project(rel, h):
        x = nrm[2 * rel : 2 * rel + 2, pl.ds(pl.multiple_of(h * part_rows, part_rows), part_rows), :]
        x = x.reshape(2 * part_rows, dim)

        def tab(ref, b):
            off = pl.multiple_of((2 * rel + b) * rows + h * part_rows, part_rows)
            return ref[pl.ds(off, part_rows), :]

        def turned(v, b):
            return (v * tab(ct, b) + pltpu.roll(v, HD // 2, 1) * tab(st, b)).astype(BF16)

        for n in range(3):
            y = jnp.dot(x, wq[:, 2 * n * HD : 2 * (n + 1) * HD], preferred_element_type=F32)
            for b in range(2):
                yb = y[b * part_rows : (b + 1) * part_rows]
                if n < 2:
                    for k in range(2):
                        at = (2 * n + k) * part_rows
                        qb[rel, b, h, at : at + part_rows, :] = turned(yb[:, k * HD : (k + 1) * HD], b)
                else:
                    off = pl.multiple_of((2 * rel + b) * rows + h * part_rows, part_rows)
                    kb[pl.ds(off, part_rows), :] = turned(yb[:, :HD], b)
                    vb[pl.ds(off, part_rows), :] = yb[:, HD:].astype(BF16)

    factor = np.float32(math.log2(math.e) / math.sqrt(HD))

    def att_copy(rel, r):
        k = 4 * rel + r
        return remote(att.at[0, rel, r], att.at[1, rel, r], at_s.at[k], at_r.at[k], mate)

    def attend(rel, r):
        b, h = r // 2 if isinstance(r, int) else lax.div(r, 2), r % 2 if isinstance(r, int) else lax.rem(r, 2)
        side = 1 - hi if rel else hi
        q = qb[rel, b, h]
        nt = (((1,), (1,)), ((), ()))
        sc = lax.dot_general(q, kv[:, :HD], nt, preferred_element_type=F32) + bias[...]
        sn = lax.dot_general(q, kb[...], nt, preferred_element_type=F32)
        kid = lax.broadcasted_iota(jnp.int32, (1, 4 * rows), 1)
        kpos = jnp.where(kid < 2 * rows, kid + 2 * rows * hi, kid - 2 * rows * hi)
        qid = lax.rem(lax.broadcasted_iota(jnp.int32, (GROUP * part_rows, 1), 0), part_rows)
        qpos = qid + (2 * rows * side + rows * b + part_rows * h)
        sn = jnp.where(kpos <= qpos, sn, -jnp.inf)
        m = jnp.maximum(jnp.max(sc, -1, keepdims=True), jnp.max(sn, -1, keepdims=True))
        ec = jnp.exp2((sc - m) * factor)
        en = jnp.exp2((sn - m) * factor)
        total = jnp.sum(ec, -1, keepdims=True) + jnp.sum(en, -1, keepdims=True)
        o = jnp.dot(ec.astype(BF16), kv[:, HD:], preferred_element_type=F32)
        o = o + jnp.dot(en.astype(BF16), vb[...], preferred_element_type=F32)
        o = (o / total).astype(BF16)
        for k in range(GROUP):
            att[0, rel, r, :, k * HD : (k + 1) * HD] = o[k * part_rows : (k + 1) * part_rows]
        att_copy(rel, r).start()

    tile = wide // 4

    def output(rel, r):
        att_copy(rel, r).wait_recv()
        at = pl.ds(pl.multiple_of(r * part_rows, part_rows), part_rows)
        b, h = lax.div(r, 2), lax.rem(r, 2)
        inner = pl.ds(pl.multiple_of(h * part_rows, part_rows), part_rows)
        for n in range(4):
            cols = slice(n * tile, (n + 1) * tile)
            y = jnp.dot(att[0, rel, r], wo[0, :, cols], preferred_element_type=F32)
            y = y + jnp.dot(att[1, rel, r], wo[1, :, cols], preferred_element_type=F32)
            if rel:
                snd[at, cols] = y.astype(BF16)
            else:
                y = y + res[b, inner, cols].astype(F32)
                base[at, cols] = y

                @pl.when(special)
                def _():
                    bsnd[at, cols] = y.astype(BF16)

        if rel:
            for i in range(per):
                sum_copy(r * per + i).start()
        else:

            @pl.when(special)
            def _():
                base_copy(r).start()

    def piece(f):
        return pl.ds(pl.multiple_of(f * PIECE, PIECE), PIECE)

    def sum_copy(f):
        return remote(snd.at[piece(f)], rcv.at[piece(f)], rs_s.at[f], rs_r.at[f], sum_dev)

    def base_copy(r):
        at = pl.ds(pl.multiple_of(r * part_rows, part_rows), part_rows)
        return remote(bsnd.at[at], brcv.at[at], bs_s.at[r], bs_r.at[r], base_dev)

    in_block = 2 * per

    def x_copy(f):
        b, k = lax.div(f, in_block), lax.rem(f, in_block)
        return remote(
            fin.at[piece(f)], out.at[0, piece(k), mine], x_s.at[f], x_r.at[c * in_block + k], (nxt, 2 * hi + b)
        )

    def finish(f):
        sum_copy(f).wait_recv()

        @pl.when(special)
        def _():
            @pl.when(lax.rem(f, per) == 0)
            def _():
                base_copy(lax.div(f, per)).wait_recv()

            fin[piece(f), :] = (brcv[piece(f), :].astype(F32) + rcv[piece(f), :].astype(F32)).astype(BF16)

        @pl.when(jnp.logical_not(special))
        def _():
            fin[piece(f), :] = (base[piece(f), :] + rcv[piece(f), :].astype(F32)).astype(BF16)

        x_copy(f).start()

    for j in range(AG):
        mate_arrival(j).wait_recv()
    wq_cp.wait()

    def own_projection(h, _):
        project(0, h)
        return 0

    lax.fori_loop(0, 2, own_projection, 0)
    kv_cp.wait()

    for j in range(AG // 2):
        ag_copy(j).wait_recv()
        fwd_copy(j).start()
    for j in range(AG // 2):
        fwd_arrival(j).wait_recv()
    project(1, 0)
    attend(1, 0)
    wo_cp.wait()
    wo_rm.wait_recv()
    res_cp.wait()
    res_in.wait_recv()
    output(1, 0)

    for j in range(AG // 2, AG):
        ag_copy(j).wait_recv()
        fwd_copy(j).start()
    for j in range(AG // 2, AG):
        fwd_arrival(j).wait_recv()
    project(1, 1)

    def step(r, _):
        attend(0, r)
        attend(1, r + 1)
        output(0, r)
        finish(2 * r)
        finish(2 * r + 1)
        output(1, r + 1)
        return 0

    lax.fori_loop(0, 3, step, 0)
    attend(0, 3)
    output(0, 3)

    def tail(f, _):
        finish(f)
        return 0

    lax.fori_loop(6, 4 * per, tail, 0)

    for j in range(AG):
        ag_copy(j).wait_send()
        mate_copy(j).wait_send()
        fwd_copy(j).wait_send()
    wo_rm.wait_send()
    res_rm.wait_send()

    def drain_att(k, _):
        remote(att.at[0, 0, 0], att.at[1, 0, 0], at_s.at[k], at_r.at[k], mate).wait_send()
        return 0

    lax.fori_loop(0, 8, drain_att, 0)

    def drain(f, _):
        sum_copy(f).wait_send()
        x_copy(f).wait_send()
        return 0

    lax.fori_loop(0, 4 * per, drain, 0)

    @pl.when(special)
    def _():
        def drain_base(r, _):
            base_copy(r).wait_send()
            return 0

        lax.fori_loop(0, 4, drain_base, 0)

    def arrive(k, _):
        side, f = lax.div(k, in_block), lax.rem(k, in_block)
        cols = pl.ds(pl.multiple_of(side * wide, wide), wide)
        remote(fin.at[piece(f)], out.at[0, piece(f), cols], x_s.at[k], x_r.at[k], mate).wait_recv()
        return 0

    lax.fori_loop(0, 2 * in_block, arrive, 0)


def split_turn():
    whole, parts = 2.0 * math.pi, []
    for _ in range(2):
        scale = 2.0 ** (math.frexp(whole)[1] - 10)
        part = math.floor(whole / scale) * scale
        parts.append(np.float32(part))
        whole -= part
    return (*parts, np.float32(whole))


TURN = split_turn()


def body(sections, acts, norm_gain, w_qkv, w_out, kv_cache, block_index, valid_len):
    rows, dim = acts.shape[1:]
    wide = dim // 2
    cached = kv_cache.shape[1]
    width = w_qkv.shape[2]
    heads = w_out.shape[1]
    exponent = 2.0 * (np.arange(HD) % (HD // 2)) / HD
    freq = jnp.asarray(np.exp(-np.log(500000.0) * exponent).astype(np.float32)[None])
    step = rows // 2
    pieces = 2 * rows // PIECE
    dma = pltpu.SemaphoreType.DMA
    smem = pl.BlockSpec(memory_space=pltpu.SMEM)
    hbm = pl.BlockSpec(memory_space=pl.ANY)
    return pl.pallas_call(
        functools.partial(kernel, sections),
        out_shape=jax.ShapeDtypeStruct((1, rows, dim), BF16),
        in_specs=[smem, smem, pl.BlockSpec(memory_space=pltpu.VMEM)] + [hbm] * 5,
        out_specs=hbm,
        scratch_shapes=[
            pltpu.VMEM((rows, dim), BF16),
            pltpu.VMEM((1, dim), F32),
            pltpu.VMEM((4, rows, dim), BF16),
            pltpu.VMEM((dim, width), BF16),
            pltpu.VMEM((2, heads, wide), BF16),
            pltpu.VMEM((cached, 2 * HD), BF16),
            pltpu.VMEM((1, cached), F32),
            pltpu.VMEM((4 * rows, HD), F32),
            pltpu.VMEM((4 * rows, HD), F32),
            pltpu.VMEM((2, 2, 2, GROUP * step, HD), BF16),
            pltpu.VMEM((4 * rows, HD), BF16),
            pltpu.VMEM((4 * rows, HD), BF16),
            pltpu.VMEM((2, 2, 4, step, heads), BF16),
            pltpu.VMEM((2, rows, wide), BF16),
            pltpu.VMEM((2 * rows, wide), F32),
            pltpu.VMEM((2 * rows, wide), BF16),
            pltpu.VMEM((2 * rows, wide), BF16),
            pltpu.VMEM((2 * rows, wide), BF16),
            pltpu.VMEM((2 * rows, wide), BF16),
            pltpu.VMEM((2 * rows, wide), BF16),
            dma((AG + 5,)),
            dma((AG,)), dma((AG,)), dma((AG,)), dma((AG,)), dma((AG,)), dma((AG,)),
            dma((2,)), dma((2,)), dma((8,)), dma((8,)),
            dma((pieces,)), dma((pieces,)), dma((4,)), dma((4,)), dma((pieces,)), dma((pieces,)),
        ],
        compiler_params=pltpu.CompilerParams(
            collective_id=0, has_side_effects=True, vmem_limit_bytes=56 * 2**20
        ),
    )(block_index, valid_len, freq, acts, norm_gain, w_qkv, w_out, kv_cache)


def solution(mesh):
    in_specs = (
        P("section", "tensor", None),
        P("section", None),
        P("section", None, "tensor"),
        P("section", "tensor", None),
        P("section", None, "tensor"),
        P("section"),
        P("section"),
    )
    out_specs = P("section", "tensor", None)
    return jax.shard_map(
        functools.partial(body, mesh.shape["section"]),
        mesh=mesh, in_specs=in_specs, out_specs=out_specs, check_vma=False,
    )
```

time: 208 us -> 86.5 us (0.42)
  waiting for transfers between devices: 154 us -> 0 us
  Pallas kernels: 0 us -> 82.8 us
  matrix products: 21.8 us -> 0 us
  between operations: 14.8 us -> 1.3 us
  other arithmetic: 12.2 us -> 0 us
    reduce_scatter x1 -> x0, waiting for transfers between devices: 82.9 us -> none  [body(): lax.psum_scatter(jnp.dot(attn, weight_out, preferred_element_type=jnp.flo...]
    pallas_call x0 -> x1, Pallas kernels: none -> 82.8 us  [body(): pl.pallas_call(functools.partial(kernel, sections), out_shape=jax.ShapeDt...]
    all_gather x1 -> x0, waiting for transfers between devices: 44.1 us -> none  [body(): lax.all_gather(normed, 'tensor', axis=0, tiled=True)]
    ppermute x1 -> x0, waiting for transfers between devices: 27.1 us -> none  [passed_along(): lax.ppermute(shard, axis, [(i, (i + by) % length) for i in range(length)])]
    dot_general x6 -> x0, matrix products: 21.8 us -> none  [the longest x1 7.76 us: body(): jnp.dot(attn, weight_out, preferred_element_type=jnp.float32)]
    reduce_sum x3 -> x0, other arithmetic: 4.82 us -> none  [the longest x1 2.66 us: body(): jnp.sum(e_cache, -1, keepdims=True) + jnp.sum(e_own, -1, keepdims=True)]
    convert_element_type x3 -> x0, other arithmetic: 4.34 us -> none  [the longest x1 2.53 us: body(): normed = (residual * lax.rsqrt(jnp.mean(residual * residual, -1, keepdims...]
    another operation x2 -> x0, other arithmetic: 3.03 us -> none
  transfers between devices with their start and end apart: 3 -> 0, of which waited for: 3 -> 0; matrix products, arithmetic and copies ran while one was open for 0% -> 0% of each run, Pallas kernels for 0% -> 0%
where the time goes in v1:
time: 86.5 us; the launch traced here: 86.4 us
  Pallas kernels  82.8 us (96%)
  local copies, waits for them, and re-layouts  2.29 us (3%)
  between operations  1.3 us (2%)
    pallas_call x1, Pallas kernels, body(): pl.pallas_call(functools.partial(kernel, sections), out_shape=jax.ShapeDt...  82.8 us
    unnamed x1, local copies, waits for them, and re-layouts  2.29 us

profile of v1, /device:TPU:1, one launch (start us, length us, event | category | flops | bytes accessed | tf_op | source)
XLA Modules:
  0.0 86.4 jit_solution(6974947677066025153)
XLA Ops:
  1.3 82.8 %shard_map.82 = bf16[1,128,4096]{2,1,0:T(8,128)(2,1)} custom-call(s32[1]{0:T(128)S(6)} %copy.10.bidx, s32[1]{0:T(128)S(6)} %copy.11.vlen, f32[1,128]{1,0:T(1,128)} %constant.2.clone.freq, bf16[1,128,4096]{2,1,0:T(8,128)(2,1)} %acts.1, f32[1,4096]{1,0:T(1,128)} %gain.1, bf16[1,4096,768]{2,1,0:T(8,128)(2,1)} %wqkv.1, bf16[1,512,4096]{2,1,0:T(8,128)(2,1)} %wout.1, ...), custom_call_target="tpu_custom_call" | custom-call | tf_op jit(solution)/shard_map/pallas_call | solution.py:383
  84.1 2.3 %copy.12 = bf16[1,128,4096]{2,1,0:T(8,128)(2,1)} copy(bf16[1,128,4096]{2,1,0:T(8,128)(2,1)} %shard_map.82) | data formatting | bytes 2097152

commit v2 on v1

v2 whole, which is shorter than its diff:
```python
import functools
import math

import jax
import jax.numpy as jnp
import numpy as np
from jax import lax
from jax.experimental import pallas as pl
from jax.experimental.pallas import tpu as pltpu
from jax.sharding import PartitionSpec as P

HELPERS = (30, 28, 27, 3)
GROUP = 4
HD = 128
AG = 4
PIECE = 16
MESH = pl.DeviceIdType.MESH
F32 = jnp.float32
BF16 = jnp.bfloat16


def kernel(
    sections, bidx_in, vlen_in, freq_in, acts, gain, wqkv, wout, cache, out,
    bidx, vlen, freq, a_v, g_v, nrm, wq, wo, kall, vall, bias, ct, st, qb, acc, top, total, att, res, base, snd, rcv, bsnd, brcv, fin, relay,
    l_sem, ag_s, ag_r, mt_s, mt_r, fw_s, fw_r, wo_s, wo_r, at_s, at_r, rs_s, rs_r, bs_s, bs_r, x_s, x_r, ro_s, ro_r, ri_s, ri_r,
):
    rows, dim = a_v.shape
    wide = dim // 2
    chunk = rows // AG
    part = rows // 2
    per = part // PIECE
    half = sections // 2
    cached = cache.shape[1]
    heads = wout.shape[1]
    pieces = 4 * per

    s = lax.axis_index("section")
    t = lax.axis_index("tensor")
    c = lax.rem(t, 2)
    hi = lax.div(t, 2)
    low = lax.rem(s, half)
    last = lax.div(low, half - 1)
    nxt = s - low + lax.rem(low + 1, half)
    prv = s - low + lax.rem(low + half - 1, half)
    oth = lax.rem(s + half, sections)
    mate = (s, 2 * hi + 1 - c)
    partner = (s, 2 * (1 - hi) + c)
    sum_dev = (lax.rem(s + half * last, sections), 2 * (1 - hi) + c)
    base_dev = (oth, t)
    first = s - low
    ends = first + half - 1
    helper = [low == k for k in HELPERS]
    relays = functools.reduce(jnp.logical_or, helper)
    quarter = sum(jnp.where(helper[q], q, 0) for q in range(1, len(HELPERS)))
    cross_dev = (oth, 2 * (1 - hi) + c)
    special = last == 1

    def remote(src, dst, ss, rs, dev):
        return pltpu.make_async_remote_copy(
            src_ref=src, dst_ref=dst, send_sem=ss, recv_sem=rs, device_id=dev, device_id_type=MESH
        )

    def span(start, size):
        return pl.ds(pl.multiple_of(start, size), size)

    mine = span(c * wide, wide)
    others = span((1 - c) * wide, wide)
    g_cp = pltpu.make_async_copy(gain, g_v, l_sem.at[AG])
    a_cp = [
        pltpu.make_async_copy(
            acts.at[0, pl.ds(j * chunk, chunk)], a_v.at[pl.ds(j * chunk, chunk)], l_sem.at[j]
        )
        for j in range(AG)
    ]
    a_cp[0].start()
    g_cp.start()
    small = [
        pltpu.make_async_copy(src, dst, l_sem.at[AG + 6 + i])
        for i, (src, dst) in enumerate(((bidx_in, bidx), (vlen_in, vlen), (freq_in, freq)))
    ]
    for j in range(1, AG):
        a_cp[j].start()

    barrier = pltpu.get_barrier_semaphore()
    for dev in (partner, mate, (prv, 2 * hi), (prv, 2 * hi + 1)):
        pl.semaphore_signal(barrier, inc=1, device_id=dev, device_id_type=MESH)

    @pl.when(special)
    def _():
        for dev in (base_dev, cross_dev, *[(first + k, t) for k in HELPERS]):
            pl.semaphore_signal(barrier, inc=1, device_id=dev, device_id_type=MESH)

    @pl.when(relays)
    def _():
        pl.semaphore_signal(barrier, inc=1, device_id=(ends, 2 * (1 - hi) + c), device_id_type=MESH)

    wq_cp = pltpu.make_async_copy(wqkv.at[0], wq, l_sem.at[AG + 1])
    k_cp = pltpu.make_async_copy(cache.at[0, :, :HD], kall.at[:cached], l_sem.at[AG + 2])
    v_cp = pltpu.make_async_copy(cache.at[0, :, HD:], vall.at[:cached], l_sem.at[AG + 3])
    wo_cp = pltpu.make_async_copy(wout.at[0, :, mine], wo.at[:heads], l_sem.at[AG + 4])
    res_cp = pltpu.make_async_copy(acts.at[0, :, mine], res.at[c], l_sem.at[AG + 5])
    wq_cp.start()
    k_cp.start()
    v_cp.start()
    for cp in small:
        cp.start()

    def ag_copy(j):
        r = span((2 * (j % 2) + c) * chunk, chunk)
        return remote(nrm.at[j // 2, r], nrm.at[2 + j // 2, r], ag_s.at[j], ag_r.at[j], partner)

    def mate_copy(k):
        r = span(k * chunk, chunk)
        return remote(nrm.at[c, r], nrm.at[c, r], mt_s.at[k], mt_r.at[k], mate)

    def mate_arrival(k):
        r = span(k * chunk, chunk)
        return remote(nrm.at[1 - c, r], nrm.at[1 - c, r], mt_s.at[k], mt_r.at[k], mate)

    def passed_on(j, core):
        slot, r = 2 + lax.div(j, 2), span((2 * lax.rem(j, 2) + core) * chunk, chunk)
        return remote(nrm.at[slot, r], nrm.at[slot, r], fw_s.at[j], fw_r.at[j], mate)

    def arrived(j):
        slot, r = 2 + lax.div(j, 2), span((2 * lax.rem(j, 2) + c) * chunk, chunk)
        return remote(nrm.at[slot, r], nrm.at[slot, r], ag_s.at[j], ag_r.at[j], partner)

    qw = dim // len(HELPERS)
    late = span((2 + c) * chunk, chunk)

    def relay_out(q):
        return remote(
            nrm.at[1, late, pl.ds(q * qw, qw)], relay, ro_s.at[q], ro_r.at[0],
            (first + HELPERS[q], 2 * (1 - hi) + c),
        )

    def relay_in():
        return remote(relay, nrm.at[3, late, span(quarter * qw, qw)], ri_s.at[0], ri_r.at[quarter], (ends, t))

    def relay_arrival(q):
        return remote(relay, nrm.at[3, late, pl.ds(q * qw, qw)], ri_s.at[0], ri_r.at[q], mate)

    g_cp.wait()
    for j in range(AG):
        a_cp[j].wait()
        r = pl.ds(j * chunk, chunk)
        x = a_v[r, :].astype(F32)
        ms = jnp.mean(x * x, -1, keepdims=True)
        nrm[c, r, :] = (x * lax.rsqrt(ms + 1e-05) * g_v[...]).astype(BF16)

    pl.semaphore_wait(barrier, 4 + (2 + len(HELPERS)) * last + jnp.where(relays, 1, 0))

    @pl.when(c == 0)
    def _():
        ag_copy(0).start()
        ag_copy(1).start()

    mate_copy(1 - c).start()
    mate_copy(3 - c).start()
    mate_arrival(c).wait_recv()
    mate_arrival(c + 2).wait_recv()

    @pl.when(c == 1)
    def _():
        ag_copy(0).start()
        ag_copy(1).start()

    ag_copy(2).start()

    @pl.when(special)
    def _():
        for q in range(len(HELPERS)):
            relay_out(q).start()

    @pl.when(jnp.logical_not(special))
    def _():
        ag_copy(3).start()

    mate_copy(c).start()
    mate_copy(c + 2).start()

    wo_cp.start()
    res_cp.start()
    wo_rm = remote(wout.at[0, :, others], wo.at[heads:], wo_s.at[0], wo_r.at[0], mate)
    res_rm = remote(acts.at[0, :, others], res.at[c], wo_s.at[1], wo_r.at[1], mate)
    res_in = remote(acts.at[0, :, mine], res.at[1 - c], wo_s.at[1], wo_r.at[1], mate)
    wo_rm.start()
    res_rm.start()

    kall[cached:, :] = jnp.zeros((4 * rows, HD), BF16)
    vall[cached:, :] = jnp.zeros((4 * rows, HD), BF16)
    for cp in small:
        cp.wait()
    lane = lax.broadcasted_iota(jnp.int32, (rows, HD), 1)
    sign = jnp.where(lane < HD // 2, -1.0, 1.0).astype(F32)
    row = lax.broadcasted_iota(jnp.int32, (rows, HD), 0)

    def tables(k, _):
        rel, b = lax.div(k, 2), lax.rem(k, 2)
        side = hi + rel - 2 * hi * rel
        pos = bidx[0] * (4 * rows) + (2 * side + b) * rows + row
        angle = pos.astype(F32) * freq[...]
        turns = jnp.floor(angle * np.float32(1.0 / (2.0 * math.pi)) + 0.5)
        angle = ((angle - turns * TURN[0]) - turns * TURN[1]) - turns * TURN[2]
        ct[span(k * rows, rows), :] = jnp.cos(angle)
        st[span(k * rows, rows), :] = jnp.sin(angle) * sign
        return 0

    lax.fori_loop(0, 4, tables, 0)
    none = F32(-jnp.inf)
    own_first = jnp.where(hi == 0, F32(0.0), none)
    other_first = jnp.where(hi == 1, F32(0.0), none)
    key_id = lax.broadcasted_iota(jnp.int32, bias.shape, 1)
    bias[...] = jnp.where(key_id < cached, jnp.where(key_id < vlen[0], F32(0.0), none), own_first)

    def project(x, rel, start, count, tiles=(2, 0, 1)):
        for n in tiles:
            y = jnp.dot(x, wq[:, 2 * n * HD : 2 * (n + 1) * HD], preferred_element_type=F32)
            for i in range(count):
                tok = span(2 * rel * rows + (start + i) * part, part)
                key_at = span(cached + 2 * rel * rows + (start + i) * part, part)
                cos, sin = ct[tok, :], st[tok, :]
                yb = y[i * part : (i + 1) * part]

                def turned(v):
                    return (v * cos + pltpu.roll(v, HD // 2, 1) * sin).astype(BF16)

                if n < 2:
                    for k in range(2):
                        at = (2 * n + k) * part
                        qb[rel, start + i, at : at + part, :] = turned(yb[:, k * HD : (k + 1) * HD])
                else:
                    kall[key_at, :] = turned(yb[:, :HD])
                    vall[key_at, :] = yb[:, HD:].astype(BF16)

    factor = np.float32(math.log2(math.e) / math.sqrt(HD))
    nt = (((1,), (1,)), ((), ()))
    near = cached + 2 * rows

    def att_copy(rel, r):
        k = 4 * rel + r
        at = span(r * part, part)
        return remote(att.at[rel, at, :heads], att.at[rel, at, heads:], at_s.at[k], at_r.at[k], mate)

    def hand_over(rel, r, o):
        at = span(r * part, part)
        for k in range(GROUP):
            att[rel, at, k * HD : (k + 1) * HD] = o[k * part : (k + 1) * part]
        att_copy(rel, r).start()

    def causal(r):
        qid = lax.rem(lax.broadcasted_iota(jnp.int32, (GROUP * part, 1), 0), part) + r * part
        return lax.broadcasted_iota(jnp.int32, (1, 2 * rows), 1) <= qid

    def softmax(sa, sb):
        m = jnp.maximum(jnp.max(sa, -1, keepdims=True), jnp.max(sb, -1, keepdims=True))
        ea = jnp.exp2((sa - m) * factor)
        eb = jnp.exp2((sb - m) * factor)
        return m, ea.astype(BF16), eb.astype(BF16), jnp.sum(ea, -1, keepdims=True) + jnp.sum(eb, -1, keepdims=True)

    def attend(r, _=0):
        q = qb[1, r]
        sa = lax.dot_general(q, kall[:near], nt, preferred_element_type=F32) + bias[...]
        sb = lax.dot_general(q, kall[near:], nt, preferred_element_type=F32)
        sb = jnp.where(causal(r), sb, none)
        _, ea, eb, tot = softmax(sa, sb)
        o = jnp.dot(ea, vall[:near], preferred_element_type=F32)
        o = o + jnp.dot(eb, vall[near:], preferred_element_type=F32)
        hand_over(1, r, (o / tot).astype(BF16))
        return 0

    def own_begin(r, _):
        q = qb[0, r]
        sa = lax.dot_general(q, kall[:cached], nt, preferred_element_type=F32) + bias[:, :cached]
        sb = lax.dot_general(q, kall[cached:near], nt, preferred_element_type=F32)
        sb = jnp.where(causal(r), sb, none)
        m, ea, eb, tot = softmax(sa, sb)
        o = jnp.dot(ea, vall[:cached], preferred_element_type=F32)
        acc[r] = o + jnp.dot(eb, vall[cached:near], preferred_element_type=F32)
        top[r] = m
        total[r] = tot
        return 0

    def own_more(r, core):
        keys = slice(near + core * rows, near + (core + 1) * rows)
        sa = lax.dot_general(qb[0, r], kall[keys], nt, preferred_element_type=F32) + other_first
        m = jnp.maximum(top[r], jnp.max(sa, -1, keepdims=True))
        scale = jnp.exp2((top[r] - m) * factor)
        ea = jnp.exp2((sa - m) * factor)
        o = acc[r] * scale + jnp.dot(ea.astype(BF16), vall[keys], preferred_element_type=F32)
        return m, total[r] * scale + jnp.sum(ea, -1, keepdims=True), o

    def own_middle(r, _):
        m, tot, o = own_more(r, 0)
        acc[r] = o
        top[r] = m
        total[r] = tot
        return 0

    def own_end(r):
        _, tot, o = own_more(r, 1)
        hand_over(0, r, (o / tot).astype(BF16))

    def piece(f):
        return span(f * PIECE, PIECE)

    def sum_copy(f):
        return remote(snd.at[piece(f)], rcv.at[piece(f)], rs_s.at[f], rs_r.at[f], sum_dev)

    def base_copy(f):
        return remote(bsnd.at[piece(f)], brcv.at[piece(f)], bs_s.at[f], bs_r.at[f], base_dev)

    def other_output(b):
        for i in range(2):
            att_copy(1, 2 * b + i).wait_recv()
        at = pl.ds(b * rows, rows)
        x = att[1, at, :]
        tile = wide // 8
        for n in range(8):
            cols = slice(n * tile, (n + 1) * tile)
            snd[at, cols] = jnp.dot(x, wo[:, cols], preferred_element_type=F32).astype(BF16)

    def send_sums(r):
        for i in range(per):
            sum_copy(r * per + i).start()

    def own_output(b):
        for i in range(2):
            att_copy(0, 2 * b + i).wait_recv()
        at = pl.ds(b * rows, rows)
        x = att[0, at, :]
        tile = wide // 8
        for n in range(8):
            cols = slice(n * tile, (n + 1) * tile)
            y = jnp.dot(x, wo[:, cols], preferred_element_type=F32)
            base[at, cols] = y + res[b, :, cols].astype(F32)

        @pl.when(special)
        def _():
            bsnd[at, :] = base[at, :].astype(BF16)
            for i in range(2 * per):
                base_copy(2 * b * per + i).start()

    in_block = 2 * per

    def x_copy(f):
        b, k = lax.div(f, in_block), lax.rem(f, in_block)
        return remote(
            fin.at[piece(f)], out.at[0, piece(k), mine], x_s.at[f], x_r.at[c * in_block + k], (nxt, 2 * hi + b)
        )

    def finish(f, _):
        sum_copy(f).wait_recv()

        @pl.when(special)
        def _():
            base_copy(f).wait_recv()
            fin[piece(f), :] = (brcv[piece(f), :].astype(F32) + rcv[piece(f), :].astype(F32)).astype(BF16)

        @pl.when(jnp.logical_not(special))
        def _():
            fin[piece(f), :] = (base[piece(f), :] + rcv[piece(f), :].astype(F32)).astype(BF16)

        x_copy(f).start()
        return 0

    def other_rows(j):
        return nrm[2 + lax.div(j, 2), span(lax.rem(j, 2) * part, part), :]

    mate_arrival(1 - c).wait_recv()
    mate_arrival(3 - c).wait_recv()
    wq_cp.wait()
    project(nrm[0:2].reshape(2 * rows, dim), 0, 0, 4)
    k_cp.wait()
    v_cp.wait()
    lax.fori_loop(0, 4, own_begin, 0)
    wo_cp.wait()
    wo_rm.wait_recv()
    res_cp.wait()
    res_in.wait_recv()

    for j in range(2):
        arrived(j).wait_recv()
        passed_on(j, c).start()

    @pl.when(relays)
    def _():
        relay_out(0).wait_recv()
        relay_in().start()

    for j in range(2):
        passed_on(j, 1 - c).wait_recv()
    project(nrm[2], 1, 0, 2)
    lax.fori_loop(0, 2, attend, 0)
    lax.fori_loop(0, 4, own_middle, 0)
    other_output(0)

    @pl.when(jnp.logical_not(special))
    def _():
        send_sums(0)
        send_sums(1)

    arrived(2).wait_recv()
    passed_on(2, c).start()
    passed_on(2, 1 - c).wait_recv()
    project(other_rows(2), 1, 2, 1)
    attend(2)

    @pl.when(special)
    def _():
        for q in range(len(HELPERS)):
            relay_arrival(q).wait_recv()

        def held(r, _):
            send_sums(r)
            return 0

        lax.fori_loop(0, 2, held, 0)

    @pl.when(jnp.logical_not(special))
    def _():
        arrived(3).wait_recv()

    passed_on(3, c).start()
    passed_on(3, 1 - c).wait_recv()
    project(other_rows(3), 1, 3, 1, (2,))
    own_end(0)
    own_end(1)
    project(other_rows(3), 1, 3, 1, (0, 1))
    own_output(0)
    finish(0, 0)
    finish(1, 0)
    own_end(2)
    own_end(3)
    attend(3)
    finish(2, 0)
    own_output(1)
    finish(3, 0)
    other_output(1)
    send_sums(2)
    send_sums(3)
    lax.fori_loop(4, pieces, finish, 0)

    for j in range(AG):
        if j < 3:
            ag_copy(j).wait_send()
        mate_copy(j).wait_send()
        passed_on(j, c).wait_send()

    @pl.when(special)
    def _():
        for q in range(len(HELPERS)):
            relay_out(q).wait_send()

    @pl.when(jnp.logical_not(special))
    def _():
        ag_copy(3).wait_send()

    @pl.when(relays)
    def _():
        relay_in().wait_send()

    wo_rm.wait_send()
    res_rm.wait_send()
    for rel in range(2):
        for r in range(4):
            att_copy(rel, r).wait_send()

    def drain(f, _):
        sum_copy(f).wait_send()
        x_copy(f).wait_send()
        return 0

    lax.fori_loop(0, pieces, drain, 0)

    @pl.when(special)
    def _():
        def drain_base(f, _):
            base_copy(f).wait_send()
            return 0

        lax.fori_loop(0, pieces, drain_base, 0)

    def arrive(k, _):
        side, f = lax.div(k, in_block), lax.rem(k, in_block)
        cols = span(side * wide, wide)
        remote(fin.at[piece(f)], out.at[0, piece(f), cols], x_s.at[k], x_r.at[k], mate).wait_recv()
        return 0

    lax.fori_loop(0, 2 * in_block, arrive, 0)


def split_turn():
    whole, parts = 2.0 * math.pi, []
    for _ in range(2):
        scale = 2.0 ** (math.frexp(whole)[1] - 10)
        part = math.floor(whole / scale) * scale
        parts.append(np.float32(part))
        whole -= part
    return (*parts, np.float32(whole))


TURN = split_turn()


def body(sections, acts, norm_gain, w_qkv, w_out, kv_cache, block_index, valid_len):
    rows, dim = acts.shape[1:]
    wide = dim // 2
    cached = kv_cache.shape[1]
    width = w_qkv.shape[2]
    heads = w_out.shape[1]
    exponent = 2.0 * (np.arange(HD) % (HD // 2)) / HD
    freq = jnp.asarray(np.exp(-np.log(500000.0) * exponent).astype(np.float32)[None])
    step = rows // 2
    pieces = 2 * rows // PIECE
    keys = cached + 4 * rows
    dma = pltpu.SemaphoreType.DMA
    hbm = pl.BlockSpec(memory_space=pltpu.HBM)
    return pl.pallas_call(
        functools.partial(kernel, sections),
        out_shape=pltpu.VMEM((1, rows, dim), BF16),
        in_specs=[hbm] * 8,
        out_specs=pl.BlockSpec(memory_space=pltpu.VMEM),
        scratch_shapes=[
            pltpu.SMEM((1,), jnp.int32),
            pltpu.SMEM((1,), jnp.int32),
            pltpu.VMEM((1, HD), F32),
            pltpu.VMEM((rows, dim), BF16),
            pltpu.VMEM((1, dim), F32),
            pltpu.VMEM((4, rows, dim), BF16),
            pltpu.VMEM((dim, width), BF16),
            pltpu.VMEM((2 * heads, wide), BF16),
            pltpu.VMEM((keys, HD), BF16),
            pltpu.VMEM((keys, HD), BF16),
            pltpu.VMEM((1, cached + 2 * rows), F32),
            pltpu.VMEM((4 * rows, HD), F32),
            pltpu.VMEM((4 * rows, HD), F32),
            pltpu.VMEM((2, 4, GROUP * step, HD), BF16),
            pltpu.VMEM((4, GROUP * step, HD), F32),
            pltpu.VMEM((4, GROUP * step, 1), F32),
            pltpu.VMEM((4, GROUP * step, 1), F32),
            pltpu.VMEM((2, 2 * rows, 2 * heads), BF16),
            pltpu.VMEM((2, rows, wide), BF16),
            pltpu.VMEM((2 * rows, wide), F32),
            pltpu.VMEM((2 * rows, wide), BF16),
            pltpu.VMEM((2 * rows, wide), BF16),
            pltpu.VMEM((2 * rows, wide), BF16),
            pltpu.VMEM((2 * rows, wide), BF16),
            pltpu.VMEM((2 * rows, wide), BF16),
            pltpu.VMEM((rows // AG, dim // len(HELPERS)), BF16),
            dma((AG + 9,)),
            dma((AG,)), dma((AG,)), dma((AG,)), dma((AG,)), dma((AG,)), dma((AG,)),
            dma((2,)), dma((2,)), dma((8,)), dma((8,)),
            dma((pieces,)), dma((pieces,)), dma((pieces,)), dma((pieces,)), dma((pieces,)), dma((pieces,)),
            dma((len(HELPERS),)), dma((1,)), dma((1,)), dma((len(HELPERS),)),
        ],
        compiler_params=pltpu.CompilerParams(
            collective_id=0, has_side_effects=True, vmem_limit_bytes=56 * 2**20
        ),
    )(block_index, valid_len, freq, acts, norm_gain, w_qkv, w_out, kv_cache)

def solution(mesh):
    in_specs = (
        P("section", "tensor", None),
        P("section", None),
        P("section", None, "tensor"),
        P("section", "tensor", None),
        P("section", None, "tensor"),
        P("section"),
        P("section"),
    )
    out_specs = P("section", "tensor", None)
    return jax.shard_map(
        functools.partial(body, mesh.shape["section"]),
        mesh=mesh, in_specs=in_specs, out_specs=out_specs, check_vma=False,
    )
```

time: 86.5 us -> 74.6 us (0.86)
  Pallas kernels: 82.8 us -> 72.2 us
  local copies, waits for them, and re-layouts: 2.29 us -> 0.97 us
    pallas_call x1, Pallas kernels: 82.8 us -> 72.2 us  [body(): pl.pallas_call(functools.partial(kernel, sections), out_shape=pltpu.VMEM(...]
    unnamed x1, local copies, waits for them, and re-layouts: 2.29 us -> 0.97 us
where the time goes in v2:
time: 74.6 us; the launch traced here: 74.5 us
  Pallas kernels  72.2 us (97%)
  between operations  1.3 us (2%)
  local copies, waits for them, and re-layouts  0.97 us (1%)
    pallas_call x1, Pallas kernels, body(): pl.pallas_call(functools.partial(kernel, sections), out_shape=pltpu.VMEM(...  72.2 us

profile of v2, /device:TPU:1, one launch (start us, length us, event | category | flops | bytes accessed | tf_op | source)
XLA Modules:
  0.0 74.5 jit_solution(15512612857983379549)
XLA Ops:
  1.3 72.2 %shard_map.82 = bf16[1,128,4096]{2,1,0:T(8,128)(2,1)S(1)} custom-call(s32[1]{0:T(128)S(6)} %copy.11.bidx_in, s32[1]{0:T(128)S(6)} %copy.12.vlen_in, f32[1,128]{1,0:T(1,128)} %constant.2.clone.freq_in, bf16[1,128,4096]{2,1,0:T(8,128)(2,1)} %acts.1, f32[1,4096]{1,0:T(1,128)} %gain.1, bf16[1,4096,768]{2,1,0:T(8,128)(2,1)} %wqkv.1, bf16[1,512,4096]{2,1,0:T(8,128)(2,1)} %wout.1, ...), custom_call_target="tpu_custom_call" | custom-call | tf_op jit(solution)/shard_map/pallas_call | solution.py:519
  73.5 1.0 %copy.10 = bf16[1,128,4096]{2,1,0:T(8,128)(2,1)} copy(bf16[1,128,4096]{2,1,0:T(8,128)(2,1)S(1)} %shard_map.82) | data formatting | bytes 2097152

commit v3 on v2

--- a/solution.py
+++ b/solution.py
@@ -9,7 +9,7 @@
 from jax.experimental.pallas import tpu as pltpu
 from jax.sharding import PartitionSpec as P
 
-HELPERS = (30, 28, 27, 3)
+HELPERS = (30, 27, 26, 23)
 GROUP = 4
 HD = 128
 AG = 4
@@ -364,9 +364,6 @@
         x_copy(f).start()
         return 0
 
-    def other_rows(j):
-        return nrm[2 + lax.div(j, 2), span(lax.rem(j, 2) * part, part), :]
-
     mate_arrival(1 - c).wait_recv()
     mate_arrival(3 - c).wait_recv()
     wq_cp.wait()
@@ -394,47 +391,37 @@
     lax.fori_loop(0, 2, attend, 0)
     lax.fori_loop(0, 4, own_middle, 0)
     other_output(0)
-
-    @pl.when(jnp.logical_not(special))
-    def _():
-        send_sums(0)
-        send_sums(1)
+    send_sums(0)
+    send_sums(1)
 
     arrived(2).wait_recv()
     passed_on(2, c).start()
-    passed_on(2, 1 - c).wait_recv()
-    project(other_rows(2), 1, 2, 1)
-    attend(2)
 
     @pl.when(special)
     def _():
         for q in range(len(HELPERS)):
             relay_arrival(q).wait_recv()
 
-        def held(r, _):
-            send_sums(r)
-            return 0
-
-        lax.fori_loop(0, 2, held, 0)
-
     @pl.when(jnp.logical_not(special))
     def _():
         arrived(3).wait_recv()
 
     passed_on(3, c).start()
+    passed_on(2, 1 - c).wait_recv()
     passed_on(3, 1 - c).wait_recv()
-    project(other_rows(3), 1, 3, 1, (2,))
+    project(nrm[3], 1, 2, 2, (2,))
     own_end(0)
     own_end(1)
-    project(other_rows(3), 1, 3, 1, (0, 1))
+    project(nrm[3], 1, 2, 2, (0, 1))
     own_output(0)
     finish(0, 0)
     finish(1, 0)
     own_end(2)
     own_end(3)
-    attend(3)
+    attend(2)
     finish(2, 0)
     own_output(1)
+    attend(3)
     finish(3, 0)
     other_output(1)
     send_sums(2)

time: 74.6 us -> 72.6 us (0.973)
  Pallas kernels: 72.2 us -> 70.2 us
    pallas_call x1, Pallas kernels: 72.2 us -> 70.2 us  [body(): pl.pallas_call(functools.partial(kernel, sections), out_shape=pltpu.VMEM(...]
where the time goes in v3:
time: 72.6 us; the launch traced here: 72.5 us
  Pallas kernels  70.2 us (97%)
  between operations  1.3 us (2%)
  local copies, waits for them, and re-layouts  0.97 us (1%)
    pallas_call x1, Pallas kernels, body(): pl.pallas_call(functools.partial(kernel, sections), out_shape=pltpu.VMEM(...  70.2 us

profile of v3, /device:TPU:1, one launch (start us, length us, event | category | flops | bytes accessed | tf_op | source)
XLA Modules:
  0.0 72.5 jit_solution(8798715944133150955)
XLA Ops:
  1.3 70.2 %shard_map.82 = bf16[1,128,4096]{2,1,0:T(8,128)(2,1)S(1)} custom-call(s32[1]{0:T(128)S(6)} %copy.11.bidx_in, s32[1]{0:T(128)S(6)} %copy.12.vlen_in, f32[1,128]{1,0:T(1,128)} %constant.2.clone.freq_in, bf16[1,128,4096]{2,1,0:T(8,128)(2,1)} %acts.1, f32[1,4096]{1,0:T(1,128)} %gain.1, bf16[1,4096,768]{2,1,0:T(8,128)(2,1)} %wqkv.1, bf16[1,512,4096]{2,1,0:T(8,128)(2,1)} %wout.1, ...), custom_call_target="tpu_custom_call" | custom-call | tf_op jit(solution)/shard_map/pallas_call | solution.py:506
  71.5 1.0 %copy.10 = bf16[1,128,4096]{2,1,0:T(8,128)(2,1)} copy(bf16[1,128,4096]{2,1,0:T(8,128)(2,1)S(1)} %shard_map.82) | data formatting | bytes 2097152

commit v4 on v3

--- a/solution.py
+++ b/solution.py
@@ -126,19 +126,26 @@
         return remote(nrm.at[slot, r], nrm.at[slot, r], ag_s.at[j], ag_r.at[j], partner)
 
     qw = dim // len(HELPERS)
-    late = span((2 + c) * chunk, chunk)
-
-    def relay_out(q):
+    ways = len(HELPERS)
+
+    def late(i):
+        return span((2 * i + c) * chunk, chunk)
+
+    def relay_out(q, i):
         return remote(
-            nrm.at[1, late, pl.ds(q * qw, qw)], relay, ro_s.at[q], ro_r.at[0],
+            nrm.at[1, late(i), pl.ds(q * qw, qw)], relay.at[i], ro_s.at[i * ways + q], ro_r.at[i],
             (first + HELPERS[q], 2 * (1 - hi) + c),
         )
 
-    def relay_in():
-        return remote(relay, nrm.at[3, late, span(quarter * qw, qw)], ri_s.at[0], ri_r.at[quarter], (ends, t))
-
-    def relay_arrival(q):
-        return remote(relay, nrm.at[3, late, pl.ds(q * qw, qw)], ri_s.at[0], ri_r.at[q], mate)
+    def relay_in(i):
+        return remote(
+            relay.at[i], nrm.at[3, late(i), span(quarter * qw, qw)], ri_s.at[i], ri_r.at[i * ways + quarter], (ends, t)
+        )
+
+    def relay_arrival(q, i):
+        return remote(
+            relay.at[i], nrm.at[3, late(i), pl.ds(q * qw, qw)], ri_s.at[i], ri_r.at[i * ways + q], mate
+        )
 
     g_cp.wait()
     for j in range(AG):
@@ -165,15 +172,15 @@
         ag_copy(0).start()
         ag_copy(1).start()
 
-    ag_copy(2).start()
-
     @pl.when(special)
     def _():
-        for q in range(len(HELPERS)):
-            relay_out(q).start()
+        for i in range(2):
+            for q in range(len(HELPERS)):
+                relay_out(q, i).start()
 
     @pl.when(jnp.logical_not(special))
     def _():
+        ag_copy(2).start()
         ag_copy(3).start()
 
     mate_copy(c).start()
@@ -382,8 +389,9 @@
 
     @pl.when(relays)
     def _():
-        relay_out(0).wait_recv()
-        relay_in().start()
+        for i in range(2):
+            relay_out(0, i).wait_recv()
+            relay_in(i).start()
 
     for j in range(2):
         passed_on(j, 1 - c).wait_recv()
@@ -394,19 +402,19 @@
     send_sums(0)
     send_sums(1)
 
-    arrived(2).wait_recv()
-    passed_on(2, c).start()
-
-    @pl.when(special)
-    def _():
-        for q in range(len(HELPERS)):
-            relay_arrival(q).wait_recv()
-
-    @pl.when(jnp.logical_not(special))
-    def _():
-        arrived(3).wait_recv()
-
-    passed_on(3, c).start()
+    for i in range(2):
+
+        @pl.when(special)
+        def _():
+            for q in range(len(HELPERS)):
+                relay_arrival(q, i).wait_recv()
+
+        @pl.when(jnp.logical_not(special))
+        def _():
+            arrived(2 + i).wait_recv()
+
+        passed_on(2 + i, c).start()
+
     passed_on(2, 1 - c).wait_recv()
     passed_on(3, 1 - c).wait_recv()
     project(nrm[3], 1, 2, 2, (2,))
@@ -429,23 +437,26 @@
     lax.fori_loop(4, pieces, finish, 0)
 
     for j in range(AG):
-        if j < 3:
+        if j < 2:
             ag_copy(j).wait_send()
         mate_copy(j).wait_send()
         passed_on(j, c).wait_send()
 
     @pl.when(special)
     def _():
-        for q in range(len(HELPERS)):
-            relay_out(q).wait_send()
+        for i in range(2):
+            for q in range(len(HELPERS)):
+                relay_out(q, i).wait_send()
 
     @pl.when(jnp.logical_not(special))
     def _():
+        ag_copy(2).wait_send()
         ag_copy(3).wait_send()
 
     @pl.when(relays)
     def _():
-        relay_in().wait_send()
+        for i in range(2):
+            relay_in(i).wait_send()
 
     wo_rm.wait_send()
     res_rm.wait_send()
@@ -534,12 +545,12 @@
             pltpu.VMEM((2 * rows, wide), BF16),
             pltpu.VMEM((2 * rows, wide), BF16),
             pltpu.VMEM((2 * rows, wide), BF16),
-            pltpu.VMEM((rows // AG, dim // len(HELPERS)), BF16),
+            pltpu.VMEM((2, rows // AG, dim // len(HELPERS)), BF16),
             dma((AG + 9,)),
             dma((AG,)), dma((AG,)), dma((AG,)), dma((AG,)), dma((AG,)), dma((AG,)),
             dma((2,)), dma((2,)), dma((8,)), dma((8,)),
             dma((pieces,)), dma((pieces,)), dma((pieces,)), dma((pieces,)), dma((pieces,)), dma((pieces,)),
-            dma((len(HELPERS),)), dma((1,)), dma((1,)), dma((len(HELPERS),)),
+            dma((2 * len(HELPERS),)), dma((2,)), dma((2,)), dma((2 * len(HELPERS),)),
         ],
         compiler_params=pltpu.CompilerParams(
             collective_id=0, has_side_effects=True, vmem_limit_bytes=56 * 2**20

time: 72.6 us -> 73 us (level)
  no operation moved by 1% of the time
where the time goes in v4:
time: 73 us; the launch traced here: 72.9 us
  Pallas kernels  70.6 us (97%)
  between operations  1.3 us (2%)
  local copies, waits for them, and re-layouts  0.97 us (1%)
    pallas_call x1, Pallas kernels, body(): pl.pallas_call(functools.partial(kernel, sections), out_shape=pltpu.VMEM(...  70.6 us

profile of v4, /device:TPU:1, one launch (start us, length us, event | category | flops | bytes accessed | tf_op | source)
XLA Modules:
  0.0 72.9 jit_solution(5063515765550410915)
XLA Ops:
  1.3 70.6 %shard_map.82 = bf16[1,128,4096]{2,1,0:T(8,128)(2,1)S(1)} custom-call(s32[1]{0:T(128)S(6)} %copy.11.bidx_in, s32[1]{0:T(128)S(6)} %copy.12.vlen_in, f32[1,128]{1,0:T(1,128)} %constant.2.clone.freq_in, bf16[1,128,4096]{2,1,0:T(8,128)(2,1)} %acts.1, f32[1,4096]{1,0:T(1,128)} %gain.1, bf16[1,4096,768]{2,1,0:T(8,128)(2,1)} %wqkv.1, bf16[1,512,4096]{2,1,0:T(8,128)(2,1)} %wout.1, ...), custom_call_target="tpu_custom_call" | custom-call | tf_op jit(solution)/shard_map/pallas_call | solution.py:517
  71.9 1.0 %copy.10 = bf16[1,128,4096]{2,1,0:T(8,128)(2,1)} copy(bf16[1,128,4096]{2,1,0:T(8,128)(2,1)S(1)} %shard_map.82) | data formatting | bytes 2097152
